TPU v7x, 32 devices: a whole 2x2x4 slice. The times are simulated.
32 devices in a mesh: member: 2 (over x), space: 16 (over z, y, core).
Axes of the slice: x: 2, y: 2, z: 4, core: 2. Of those that a mesh axis runs over, the one named last changes fastest.
Arguments:
- params: float32 [256, 64, 1024], P('member', 'space'), may hold values from -2 to 2
- state: float32 [256, 64, 1024], P('member', 'space'), may hold values from -6 to 6
- regime: int32 [64, 1024], P('space'), may hold values from 0 to 7
- regime_coefs: float32 [8, 4], replicated, may hold values from 0.1 to 0.5
- observation_index: int32 [8192], P('space'), may hold values from 0 to 65535, as said below
- measured_values: float32 [8192], P('space'), may hold values from -6 to 6
- observation_spread: float32 [8192], P('space'), may hold values from 0.1 to 1
- observation_jitter: float32 [256, 8192], P('member', 'space'), may hold values from -6 to 6
Outputs:
- revised_log_diffusivity: float32 [256, 64, 1024], P('member', 'space')
- predicted_member_state: float32 [256, 64, 1024], P('member', 'space')
Inputs may be any that keep to these rules, and one draw needn't show every extreme that they name: `observation_index`: observation o lies in the strip of rows o // 512 * 4 up to (o // 512 + 1) * 4 - 1; the first observation of each strip sits on its first cell, the second on its last cell; cells may repeat.
All inputs are finite; a program needn't handle non-finite values.
Results may differ from a plain program's by a relative error of at most 0.015.
Values sent between devices are 32-bit elements; how exact they have to be, the bound alone decides.
A program may use at most 64 MiB of HBM per device.

v0:
```python
import math

import jax
import jax.numpy as jnp
from jax import lax
from jax.sharding import PartitionSpec as P

time_step = 0.06


def with_halo(cells, sides, width):
    for axis, dim in sides:
        count = lax.axis_size(axis)
        ends = count - 1
        head = lax.slice_in_dim(cells, 0, width, axis=dim)
        tail = lax.slice_in_dim(cells, cells.shape[dim] - width, cells.shape[dim], axis=dim)
        cells = jnp.concatenate(
            [
                lax.ppermute(tail, axis, [(i, (i + 1) % count) for i in range(ends)]),
                cells,
                lax.ppermute(head, axis, [((i + 1) % count, i) for i in range(ends)]),
            ],
            axis=dim,
        )
    return cells


def coef_fields(regime, regime_coefs):
    levels = jnp.arange(regime_coefs.shape[0], dtype=jnp.int32)
    onehot = (regime[None, :, :] == levels[:, None, None]).astype(jnp.float32)
    return jnp.einsum("rd,rxy->dxy", regime_coefs, onehot, precision=lax.Precision.HIGHEST)


def advance(extended, rates, coefs):
    center = extended[..., 1:-1, :]
    widths = [(0, 0)] * (center.ndim - 1) + [(1, 1)]
    padded_cols = jnp.pad(center, widths)
    above = extended[..., :-2, :]
    below = extended[..., 2:, :]
    left_side = padded_cols[..., :-2]
    right_side = padded_cols[..., 2:]
    flow = coefs[0] * (above - center) + coefs[1] * (below - center)
    flow = flow + coefs[2] * (left_side - center) + coefs[3] * (right_side - center)
    return center + rates * flow


def body(
    params,
    state,
    regime,
    regime_coefs,
    observation_index,
    measured_values,
    observation_spread,
    observation_jitter,
):
    block_members = params.shape[0]
    strip_rows = params.shape[1]
    columns = params.shape[2]
    member_list = block_members * lax.axis_size("member")
    square_root_scale = math.sqrt(member_list - 1)
    coefs = coef_fields(regime, regime_coefs)
    rates = time_step * jnp.exp(params)
    current = state
    for repeat in range(2):
        extended = with_halo(current, (("space", 1),), 1)
        current = advance(extended, rates, coefs)
    param_anom = params / square_root_scale
    slab_local_index = observation_index - lax.axis_index("space") * (strip_rows * columns)
    flattened_grid = current.reshape(block_members, strip_rows * columns)
    local_predictions = jnp.take(flattened_grid, slab_local_index, axis=1)
    predicted_fields, noise_draws = (
        lax.all_gather(local_predictions, "member", axis=0, tiled=True),
        lax.all_gather(observation_jitter, "member", axis=0, tiled=True),
    )
    ensemble_mean_prediction = jnp.sum(predicted_fields, axis=0) / member_list
    member_departures = (predicted_fields - ensemble_mean_prediction[None, :]) / (
        observation_spread[None, :] * square_root_scale
    )
    observation_misfits = (
        measured_values[None, :] + observation_spread[None, :] * noise_draws - predicted_fields
    ) / observation_spread[None, :]
    stacked = jnp.concatenate([member_departures, observation_misfits], axis=0)
    own_start = lax.axis_index("member") * block_members
    own_anoms = lax.dynamic_slice_in_dim(member_departures, own_start, block_members, 0)
    block_rows = jnp.dot(
        own_anoms, stacked.T, precision=lax.Precision.HIGHEST, preferred_element_type=jnp.float32
    )
    block_rows = lax.psum(block_rows, "space")
    gram_full = lax.all_gather(block_rows, "member", axis=0, tiled=True)
    gram = gram_full[:, :member_list]
    cross = gram_full[:, member_list:]
    system = jnp.eye(member_list, dtype=jnp.float32) + gram
    factor = jnp.linalg.cholesky(system)
    mixing = jax.scipy.linalg.cho_solve((factor, True), cross)
    empty = jnp.zeros(params.shape, jnp.float32)
    piece = lax.all_gather(param_anom, "member", axis=0, tiled=True)
    weights = lax.dynamic_slice(mixing, (0, own_start), (piece.shape[0], block_members))
    update = empty + jnp.einsum("kj,kxy->jxy", weights, piece, precision=lax.Precision.HIGHEST)
    revised_log_diffusivity = params + update
    return (revised_log_diffusivity, current)


def solution(mesh):
    in_specs = (
        P("member", "space", None),
        P("member", "space", None),
        P("space", None),
        P(),
        P("space"),
        P("space"),
        P("space"),
        P("member", "space"),
    )
    out_specs = (P("member", "space", None), P("member", "space", None))
    return jax.shard_map(body, mesh=mesh, in_specs=in_specs, out_specs=out_specs, check_vma=False)
```

profile of v0, /device:TPU:0, one launch (start us, length us, event | category | flops | bytes accessed | tf_op | source)
XLA Modules:
  0.0 255.9 jit_solution(9623067121630074450)
XLA Ops:
  8.1 2.8 %copy.28 = f32[128,4,1024]{2,0,1:T(8,128)S(1)} copy(f32[128,4,1024]{2,1,0:T(4,128)} %param.9) | data formatting | bytes 4194304 | tf_op args[1]
  10.9 1.3 copy-done.3
  12.2 1.0 fusion.53
  13.2 2.4 collective-permute-start
  15.6 1.3 collective-permute-start.1
  17.3 4.4 %collective-permute-done.1 = f32[128,1,1024]{2,0,1:T(8,128)S(1)} collective-permute-done((f32[128,1,1024]{2,0,1:T(8,128)}, f32[128,1,1024]{2,0,1:T(8,128)S(1)}, u32[]{:S(2)}, u32[]{:S(2)}) %collective-permute-start.1) | collective-permute-done | bytes 524320 | tf_op jit(solution)/shard_map/ppermute | solution.py:21
  21.7 5.7 %fusion.5 = f32[128,4,1024]{2,0,1:T(8,128)S(1)} fusion(f32[128,4,1024]{2,0,1:T(8,128)} %copy-done.3, f32[128,1,1024]{2,0,1:T(8,128)S(1)} %collective-permute-done.1, f32[128,1,1024]{2,0,1:T(8,128)S(1)} %collective-permute-done, f32[128,4,1024]{2,1,0:T(4,128)S(1)} %copy-done.1, f32[4,1024]{1,0:T(4,128)S(1)} %get-tuple-element.44, ...), kind=kLoop, calls=%fused_computation.12 | loop fusion | flops 8388608 | bytes 7405568 | tf_op jit(solution)/shard_map/add | solution.py:44
  27.5 1.3 copy-done.2
  28.8 1.1 fusion.52
  29.9 11.2 %collective-permute-start.2 = (f32[128,1,1024]{2,0,1:T(8,128)}, f32[128,1,1024]{2,0,1:T(8,128)}, u32[]{:S(2)}, u32[]{:S(2)}) collective-permute-start(f32[128,1,1024]{2,0,1:T(8,128)} %get-tuple-element.28), channel_id=1, source_target_pairs={{0,1},{1,2},{2,3},{3,4},{4,5},{5,6},{6,7},{7,8},{8,9},{9,10},{10,1... | collective-permute-start | bytes 1572872 | tf_op jit(solution)/shard_map/ppermute | solution.py:19
  41.1 1.3 collective-permute-start.3
  42.6 8.6 %all_gather.13 = f32[256,512]{0,1:T(8,128)S(1)} all-gather(f32[128,512]{0,1:T(8,128)S(1)} %copy.30), channel_id=1, replica_groups=mesh['member'=2,'space'=16] {'member'}, dimensions={0}, use_global_device_ids=true | all-gather | bytes 786432 | tf_op jit(solution)/shard_map/all_gather | solution.py:74
  51.2 7.4 %fusion.13 = (f32[128,4,1024]{2,0,1:T(8,128)}, f32[128,4,1024]{2,0,1:T(8,128)}) fusion(f32[128,4,1024]{2,0,1:T(8,128)} %copy-done.2, f32[128,1,1024]{2,0,1:T(8,128)} %collective-permute-done.3, f32[128,1,1024]{2,0,1:T(8,128)} %collective-permute-done.2, f32[128,4,1024]{2,1,0:T(4,128)S(1)} %copy-done.1, f32[4,1024]{1,0:T(4,128)S(1)} %get-tuple-element.44, ...), kind=kLoop, calls=%fused_computation.20 | loop fusion | flops 8912896 | bytes 9502720 | tf_op jit(solution)/shard_map/add | solution.py:44
  58.6 2.9 %copy.29 = f32[128,4,1024]{0,2,1:T(8,128)} copy(f32[128,4,1024]{2,0,1:T(8,128)} %get-tuple-element.26) | data formatting | bytes 4194304 | tf_op jit(solution)/shard_map/add | solution.py:44
  61.5 2.6 %gather_fusion = f32[512,128]{1,0:T(8,128)S(1)} fusion(f32[128,4096]{0,1:T(8,128)} %bitcast.56, s32[1024]{0:T(1024)S(1)} %pad_clamp_fusion), kind=kCustom, calls=%fused_computation | custom fusion | bytes 526336 | tf_op jit(solution)/shard_map/jit(_take)/gather | solution.py:71
  64.3 7.2 %all_gather.12 = f32[256,512]{0,1:T(8,128)S(1)} all-gather(f32[128,512]{0,1:T(8,128)S(1)} %select_bitcast_fusion), channel_id=1, replica_groups=mesh['member'=2,'space'=16] {'member'}, dimensions={0}, use_global_device_ids=true | all-gather | bytes 786432 | tf_op jit(solution)/shard_map/all_gather | solution.py:73
  72.0 2.5 fusion.26
  75.2 4.3 %copy.37 = f32[128,4,1024]{2,1,0:T(4,128)} copy(f32[128,4,1024]{2,0,1:T(8,128)} %get-tuple-element.26) | data formatting | bytes 4194304
  79.4 88.5 %all-reduce.5.cloned.1.call-done = f32[128,512]{0,1:T(8,128)} async-done(((f32[128,512]{0,1:T(8,128)}), f32[128,512]{0,1:T(8,128)}) %all-reduce.5.cloned.1.call-update) | async-done | bytes 262160 | tf_op jit(solution)/shard_map/psum | solution.py:89
  168.0 9.8 %all_gather.14 = f32[256,512]{0,1:T(8,128)S(1)} all-gather(f32[128,512]{0,1:T(8,128)} %all-reduce.5.cloned.1.call-done), channel_id=1, replica_groups=mesh['member'=2,'space'=16] {'member'}, dimensions={0}, use_global_device_ids=true | all-gather | bytes 786432 | tf_op jit(solution)/shard_map/all_gather | solution.py:90
  178.0 11.7 %cholesky.50 = f32[128,128]{1,0:T(8,128)S(1)} custom-call(f32[128,128]{1,0:T(8,128)S(1)} %cholesky.118), custom_call_target="Cholesky" | custom-call | tf_op jit(solution)/shard_map/jit(cholesky)/cholesky | solution.py:94
  189.8 9.8 %custom-call.18 = f32[1,128,128]{1,2,0:T(8,128)S(1)} custom-call(f32[1,128,128]{2,1,0:T(8,128)S(1)} %get-tuple-element.37), custom_call_target="InvertDiagBlocksLowerTriangular" | custom-call | tf_op jit(solution)/shard_map/jit(cholesky)/cholesky | solution.py:94
  200.1 11.7 %cholesky.105 = f32[128,128]{1,0:T(8,128)S(1)} custom-call(f32[128,128]{1,0:T(8,128)S(1)} %convolution_subtract_fusion.2), custom_call_target="Cholesky" | custom-call | tf_op jit(solution)/shard_map/jit(cholesky)/cholesky | solution.py:94
  211.8 0.6 compare_reduce_fusion
  212.5 0.6 compare_reduce_fusion.1
  214.4 4.0 %while.1 = (s32[]{:T(128)}, f32[256,256]{1,0:T(8,128)S(1)}, s32[2,2]{1,0:T(2,128)S(1)}, f32[2,128,128]{2,1,0:T(8,128)S(1)}, s32[]{:T(128)}) while((s32[]{:T(128)}, f32[256,256]{1,0:T(8,128)S(1)}, s32[2,2]{1,0:T(2,128)S(1)}, f32[2,128,128]{2,1,0:T(8,128)S(1)}, s32[]{:T(128)}) %tuple.38), condition=%wide.while_cond, body=%wide.while_body.sunk | while | flops 2 | bytes 131181 | solution.py:95
  215.2 1.3 bitcast_dynamic-update-slice_fusion.2
  216.5 0.6 fusion.64
  217.1 1.3 bitcast_dynamic-update-slice_fusion.2
  218.4 19.7 %custom-call.19 = f32[2,128,128]{1,2,0:T(8,128)S(1)} custom-call(f32[2,128,128]{2,1,0:T(8,128)S(1)} %get-tuple-element.9), custom_call_target="InvertDiagBlocksLowerTriangular" | custom-call | tf_op jit(solution)/shard_map/jit(_cho_solve)/triangular_solve | solution.py:95
  240.0 5.7 %copy_add_fusion = f32[128,4,1024]{2,0,1:T(8,128)S(1)} fusion(f32[128,4,1024]{2,1,0:T(4,128)S(1)} %copy-done.1, f32[256,4,1024]{2,0,1:T(8,128)} %all-gather.2.cloned.1.call-done, s32[]{:T(128)S(6)} %select_n.19, f32[128,256]{1,0:T(8,128)S(1)} %fusion.41, f32[128,256]{1,0:T(8,128)S(1)} %fusion.42), kind=kOutput, calls=%fused_computation.39 | convolution fusion | flops 1611169792 | bytes 8650756 | tf_op jit(solution)/shard_map/kj,kxy->jxy/dot_general | solution.py:99
  245.8 2.7 %copy.36 = f32[128,4,1024]{2,1,0:T(4,128)} copy(f32[128,4,1024]{2,0,1:T(8,128)S(1)} %copy_add_fusion) | data formatting | bytes 4194304
  (58 shorter events, 5.1 us)
Async XLA Ops:
  8.0 8.9 %copy-start = (f32[8,4]{0,1:T(4,128)S(1)}, f32[8,4]{0,1:T(4,128)}, u32[]{:S(2)}) copy-start(f32[8,4]{0,1:T(4,128)} %param.11) | copy-start | bytes 388
  8.0 160.0 %all-reduce.5.cloned.1.call-start = ((), (), s32[]{:S(2)}) async-start(), calls=%async_computation | async-start | bytes 524288 | tf_op jit(solution)/shard_map/psum | solution.py:89
  8.1 8.9 %copy-start.5 = (s32[4,1024]{1,0:T(4,128)S(1)}, s32[4,1024]{1,0:T(4,128)}, u32[]{:S(2)}) copy-start(s32[4,1024]{1,0:T(4,128)} %param.10) | copy-start | bytes 49156
  10.9 1.3 copy-start.3
  12.2 9.5 %copy-start.1 = (f32[128,4,1024]{2,1,0:T(4,128)S(1)}, f32[128,4,1024]{2,1,0:T(4,128)}, u32[]{:S(2)}) copy-start(f32[128,4,1024]{2,1,0:T(4,128)} %param.8) | copy-start | bytes 6291460
  13.2 4.1 %collective-permute-start = (f32[128,1,1024]{2,0,1:T(8,128)}, f32[128,1,1024]{2,0,1:T(8,128)S(1)}, u32[]{:S(2)}, u32[]{:S(2)}) collective-permute-start(f32[128,1,1024]{2,0,1:T(8,128)} %get-tuple-element.30), channel_id=1, source_target_pairs={{0,1},{1,2},{2,3},{3,4},{4,5},{5,6},{6,7},{7,8},{8,9},{9,10},{10,1... | collective-permute-start | bytes 1572872 | tf_op jit(solution)/shard_map/ppermute | solution.py:19
  15.6 6.1 %collective-permute-start.1 = (f32[128,1,1024]{2,0,1:T(8,128)}, f32[128,1,1024]{2,0,1:T(8,128)S(1)}, u32[]{:S(2)}, u32[]{:S(2)}) collective-permute-start(f32[128,1,1024]{2,0,1:T(8,128)} %get-tuple-element.31), channel_id=1, source_target_pairs={{1,0},{2,1},{3,2},{4,3},{5,4},{6,5},{7,6},{8,7},{9,8},{10,9},{11,1... | collective-permute-start | bytes 1572872 | tf_op jit(solution)/shard_map/ppermute | solution.py:21
  27.5 1.3 copy-start.2
  28.8 13.6 %copy-start.7 = (s32[512]{0:T(512)S(1)}, s32[512]{0:T(512)}, u32[]{:S(2)}) copy-start(s32[512]{0:T(512)} %param.12) | copy-start | bytes 6148
  28.8 13.6 %copy-start.4 = (f32[128,512]{1,0:T(8,128)S(1)}, f32[128,512]{1,0:T(8,128)}, u32[]{:S(2)}) copy-start(f32[128,512]{1,0:T(8,128)} %param.15) | copy-start | bytes 786436
  28.8 22.4 %copy-start.6 = (f32[512]{0:T(512)S(1)}, f32[512]{0:T(512)}, u32[]{:S(2)}) copy-start(f32[512]{0:T(512)} %param.14) | copy-start | bytes 6148
  29.9 21.3 %collective-permute-start.2 = (f32[128,1,1024]{2,0,1:T(8,128)}, f32[128,1,1024]{2,0,1:T(8,128)}, u32[]{:S(2)}, u32[]{:S(2)}) collective-permute-start(f32[128,1,1024]{2,0,1:T(8,128)} %get-tuple-element.28), channel_id=1, source_target_pairs={{0,1},{1,2},{2,3},{3,4},{4,5},{5,6},{6,7},{7,8},{8,9},{9,10},{10,1... | collective-permute-start | bytes 1572872 | tf_op jit(solution)/shard_map/ppermute | solution.py:19
  41.1 10.1 %collective-permute-start.3 = (f32[128,1,1024]{2,0,1:T(8,128)}, f32[128,1,1024]{2,0,1:T(8,128)}, u32[]{:S(2)}, u32[]{:S(2)}) collective-permute-start(f32[128,1,1024]{2,0,1:T(8,128)} %get-tuple-element.29), channel_id=1, source_target_pairs={{1,0},{2,1},{3,2},{4,3},{5,4},{6,5},{7,6},{8,7},{9,8},{10,9},{11,1... | collective-permute-start | bytes 1572872 | tf_op jit(solution)/shard_map/ppermute | solution.py:21
  61.5 10.2 %copy-start.8 = (f32[512]{0:T(512)S(1)}, f32[512]{0:T(512)}, u32[]{:S(2)}) copy-start(f32[512]{0:T(512)} %param.13) | copy-start | bytes 6148
  74.6 165.4 %all-gather.2.cloned.1.call-start = ((), (), s32[]{:S(2)}) async-start(), calls=%async_computation.1 | async-start | bytes 6291456 | tf_op jit(solution)/shard_map/all_gather | solution.py:97
Sparse Core Ops, SparseCore 0:
  74.7 93.2 all-reduce.4
Sparse Core Ops, SparseCore 1:
  76.6 61.0 all-gather.1
where the time goes:
time: 256 us
  waiting for transfers between devices  93.6 us (37%)
  other arithmetic  68.1 us (27%)
  blocking collectives  25.6 us (10%)
  local copies, waits for them, and re-layouts  24.2 us (9%)
  between operations  17.1 us (7%)
  starting transfers between devices  16.3 us (6%)
  matrix products  10.8 us (4%)
    psum x1, waiting for transfers between devices, body(): block_rows = lax.psum(block_rows, 'space')  88.5 us
    another operation x7, other arithmetic, body(): factor = jnp.linalg.cholesky(system)  34.6 us
    another operation x3, other arithmetic, body(): mixing = jax.scipy.linalg.cho_solve((factor, True), cross)  19.7 us
    ppermute x2, starting transfers between devices, with_halo(): lax.ppermute(tail, axis, [(i, (i + 1) % count) for i in range(ends)])  13.6 us
    add x2, other arithmetic, advance(): return center + rates * flow  13.1 us
    unnamed x24, local copies, waits for them, and re-layouts  12.5 us
    all_gather x1, blocking collectives, body(): gram_full = lax.all_gather(block_rows, 'member', axis=0, tiled=True)  9.8 us
    all_gather x1, blocking collectives, body(): lax.all_gather(observation_jitter, 'member', axis=0, tiled=True)  8.57 us
  transfers between devices with their start and end apart: 6, of which 3 were waited for; matrix products, arithmetic and copies ran while one was open for 26% of the time, Pallas kernels for 0%

commit v1 on v0

--- a/solution.py
+++ b/solution.py
@@ -65,40 +65,30 @@
     for repeat in range(2):
         extended = with_halo(current, (("space", 1),), 1)
         current = advance(extended, rates, coefs)
-    param_anom = params / square_root_scale
     slab_local_index = observation_index - lax.axis_index("space") * (strip_rows * columns)
     flattened_grid = current.reshape(block_members, strip_rows * columns)
-    local_predictions = jnp.take(flattened_grid, slab_local_index, axis=1)
-    predicted_fields, noise_draws = (
-        lax.all_gather(local_predictions, "member", axis=0, tiled=True),
-        lax.all_gather(observation_jitter, "member", axis=0, tiled=True),
+    own = jnp.take(flattened_grid, slab_local_index, axis=1)
+    swap = [(0, 1), (1, 0)]
+    theirs = lax.ppermute(own, "member", swap)
+    total = jnp.sum(own, axis=0) + jnp.sum(theirs, axis=0)
+    mean = total / member_list
+    fields = jnp.concatenate([own, theirs], axis=0)
+    departures = (fields - mean[None, :]) / (observation_spread[None, :] * square_root_scale)
+    misfits = (
+        measured_values[None, :] + observation_spread[None, :] * observation_jitter - own
+    ) / observation_spread[None, :]
+    stacked = jnp.concatenate([departures, misfits], axis=0)
+    rows = jnp.dot(
+        departures, stacked.T, precision=lax.Precision.HIGHEST, preferred_element_type=jnp.float32
     )
-    ensemble_mean_prediction = jnp.sum(predicted_fields, axis=0) / member_list
-    member_departures = (predicted_fields - ensemble_mean_prediction[None, :]) / (
-        observation_spread[None, :] * square_root_scale
-    )
-    observation_misfits = (
-        measured_values[None, :] + observation_spread[None, :] * noise_draws - predicted_fields
-    ) / observation_spread[None, :]
-    stacked = jnp.concatenate([member_departures, observation_misfits], axis=0)
-    own_start = lax.axis_index("member") * block_members
-    own_anoms = lax.dynamic_slice_in_dim(member_departures, own_start, block_members, 0)
-    block_rows = jnp.dot(
-        own_anoms, stacked.T, precision=lax.Precision.HIGHEST, preferred_element_type=jnp.float32
-    )
-    block_rows = lax.psum(block_rows, "space")
-    gram_full = lax.all_gather(block_rows, "member", axis=0, tiled=True)
-    gram = gram_full[:, :member_list]
-    cross = gram_full[:, member_list:]
-    system = jnp.eye(member_list, dtype=jnp.float32) + gram
+    rows = lax.psum(rows, "space")
+    params_theirs = lax.ppermute(params, "member", swap)
+    system = jnp.eye(member_list, dtype=jnp.float32) + rows[:, :member_list]
     factor = jnp.linalg.cholesky(system)
-    mixing = jax.scipy.linalg.cho_solve((factor, True), cross)
-    empty = jnp.zeros(params.shape, jnp.float32)
-    piece = lax.all_gather(param_anom, "member", axis=0, tiled=True)
-    weights = lax.dynamic_slice(mixing, (0, own_start), (piece.shape[0], block_members))
-    update = empty + jnp.einsum("kj,kxy->jxy", weights, piece, precision=lax.Precision.HIGHEST)
-    revised_log_diffusivity = params + update
-    return (revised_log_diffusivity, current)
+    mixing = jax.scipy.linalg.cho_solve((factor, True), rows[:, member_list:])
+    piece = jnp.concatenate([params, params_theirs], axis=0) / square_root_scale
+    update = jnp.einsum("kj,kxy->jxy", mixing, piece, precision=lax.Precision.HIGHEST)
+    return (params + update, current)
 
 
 def solution(mesh):

time: 256 us -> 241 us (0.941)
  blocking collectives: 25.6 us -> 0 us
  waiting for transfers between devices: 93.6 us -> 108 us
  local copies, waits for them, and re-layouts: 24.2 us -> 20.8 us
    all_gather x3 -> x0, blocking collectives: 25.6 us -> none  [the longest x1 9.8 us: body(): gram_full = lax.all_gather(block_rows, 'member', axis=0, tiled=True)]
    psum x1, waiting for transfers between devices: 88.5 us -> 94.2 us  [body(): rows = lax.psum(rows, 'space')]
    ppermute x0 -> x2, waiting for transfers between devices: none -> 4.65 us  [the longest x1 4.65 us: body(): theirs = lax.ppermute(own, 'member', swap)]
    ppermute x2, waiting for transfers between devices: 4.42 us -> 8.69 us  [with_halo(): lax.ppermute(head, axis, [((i + 1) % count, i) for i in range(ends)])]
    add x2, other arithmetic: 13.1 us -> 10 us  [advance(): return center + rates * flow]
    ppermute x0 -> x2, starting transfers between devices: none -> 3.05 us  [the longest x1 1.56 us: body(): theirs = lax.ppermute(own, 'member', swap)]
    unnamed x24 -> x22, local copies, waits for them, and re-layouts: 12.5 us -> 9.93 us
  transfers between devices with their start and end apart: 6 -> 7, of which waited for: 3 -> 5; matrix products, arithmetic and copies ran while one was open for 26% -> 29% of each run, Pallas kernels for 0% -> 0%
where the time goes in v1:
time: 241 us
  waiting for transfers between devices  108 us (45%)
  other arithmetic  67.4 us (28%)
  local copies, waits for them, and re-layouts  20.8 us (9%)
  starting transfers between devices  18.5 us (8%)
  between operations  15.6 us (6%)
  matrix products  10.3 us (4%)
    psum x1, waiting for transfers between devices, body(): rows = lax.psum(rows, 'space')  94.2 us
    another operation x7, other arithmetic, body(): factor = jnp.linalg.cholesky(system)  34.8 us
    another operation x3, other arithmetic, body(): mixing = jax.scipy.linalg.cho_solve((factor, True), rows[:, member_list:])  19.7 us
    ppermute x2, starting transfers between devices, with_halo(): lax.ppermute(tail, axis, [(i, (i + 1) % count) for i in range(ends)])  12.9 us
    add x2, other arithmetic, advance(): return center + rates * flow  10 us
    unnamed x22, local copies, waits for them, and re-layouts  9.93 us
    ppermute x2, waiting for transfers between devices, with_halo(): lax.ppermute(head, axis, [((i + 1) % count, i) for i in range(ends)])  8.69 us
  transfers between devices with their start and end apart: 7, of which 5 were waited for; matrix products, arithmetic and copies ran while one was open for 29% of the time, Pallas kernels for 0%

profile of v1, /device:TPU:0, one launch (start us, length us, event | category | flops | bytes accessed | tf_op | source)
XLA Modules:
  0.0 240.5 jit_solution(13714949432968400713)
XLA Ops:
  7.2 2.8 %copy.29 = f32[128,4,1024]{2,0,1:T(8,128)S(1)} copy(f32[128,4,1024]{2,1,0:T(4,128)} %param.9) | data formatting | bytes 4194304 | tf_op args[1]
  10.1 2.5 %collective-permute-start = (f32[128,1,1024]{2,0,1:T(8,128)S(1)}, f32[128,1,1024]{2,0,1:T(8,128)S(1)}, u32[]{:S(2)}, u32[]{:S(2)}) collective-permute-start(f32[128,1,1024]{2,0,1:T(8,128)S(1)} %get-tuple-element.32), channel_id=1, source_target_pairs={{0,1},{1,2},{2,3},{3,4},{4,5},{5,6},{6,7},{7,8},{8,9},{9,10},{10,1... | collective-permute-start | bytes 1572872 | tf_op jit(solution)/shard_map/ppermute | solution.py:19
  12.7 1.3 collective-permute-start.1
  14.3 4.3 %collective-permute-done.1 = f32[128,1,1024]{2,0,1:T(8,128)S(1)} collective-permute-done((f32[128,1,1024]{2,0,1:T(8,128)S(1)}, f32[128,1,1024]{2,0,1:T(8,128)S(1)}, u32[]{:S(2)}, u32[]{:S(2)}) %collective-permute-start.1) | collective-permute-done | bytes 524320 | tf_op jit(solution)/shard_map/ppermute | solution.py:21
  18.6 2.6 %fusion.8 = f32[128,4,1024]{2,0,1:T(8,128)S(1)} fusion(f32[128,4,1024]{2,0,1:T(8,128)S(1)} %copy.29, f32[128,1,1024]{2,0,1:T(8,128)S(1)} %collective-permute-done.1, f32[128,1,1024]{2,0,1:T(8,128)S(1)} %collective-permute-done, f32[4,1024]{1,0:T(4,128)S(1)} %get-tuple-element.44, f32[4,1024]{1,0:T(4,128)S(1)} %get-tuple-element.45, ...), kind=kLoop, calls=%fused_computation.16 | loop fusion | flops 8388608 | bytes 7405568 | tf_op jit(solution)/shard_map/add | solution.py:44
  21.2 1.1 fusion.55
  22.3 10.3 %collective-permute-start.2 = (f32[128,1,1024]{2,0,1:T(8,128)}, f32[128,1,1024]{2,0,1:T(8,128)S(1)}, u32[]{:S(2)}, u32[]{:S(2)}) collective-permute-start(f32[128,1,1024]{2,0,1:T(8,128)} %get-tuple-element.30), channel_id=1, source_target_pairs={{0,1},{1,2},{2,3},{3,4},{4,5},{5,6},{6,7},{7,8},{8,9},{9,10},{10,1... | collective-permute-start | bytes 1572872 | tf_op jit(solution)/shard_map/ppermute | solution.py:19
  32.6 1.3 collective-permute-start.3
  34.3 4.4 %collective-permute-done.3 = f32[128,1,1024]{2,0,1:T(8,128)} collective-permute-done((f32[128,1,1024]{2,0,1:T(8,128)}, f32[128,1,1024]{2,0,1:T(8,128)}, u32[]{:S(2)}, u32[]{:S(2)}) %collective-permute-start.3) | collective-permute-done | bytes 524320 | tf_op jit(solution)/shard_map/ppermute | solution.py:21
  38.7 7.5 %fusion.16 = (f32[128,4,1024]{2,0,1:T(8,128)}, f32[128,4,1024]{2,0,1:T(8,128)S(1)}) fusion(f32[128,4,1024]{2,0,1:T(8,128)} %copy-done.1, f32[128,1,1024]{2,0,1:T(8,128)} %collective-permute-done.3, f32[128,1,1024]{2,0,1:T(8,128)S(1)} %collective-permute-done.2, f32[4,1024]{1,0:T(4,128)S(1)} %get-tuple-element.44, f32[4,1024]{1,0:T(4,128)S(1)} %get-tuple-element.45, ...), kind=kLoop, calls=%fused_computation.24 | loop fusion | flops 8388608 | bytes 9502720 | tf_op jit(solution)/shard_map/add | solution.py:44
  46.2 2.9 %copy.30 = f32[128,4,1024]{0,2,1:T(8,128)} copy(f32[128,4,1024]{2,0,1:T(8,128)} %get-tuple-element.28) | data formatting | bytes 4194304 | tf_op jit(solution)/shard_map/add | solution.py:44
  49.1 2.8 %gather_fusion = f32[512,128]{1,0:T(8,128)S(1)} fusion(f32[128,4096]{0,1:T(8,128)} %bitcast.57, s32[1024]{0:T(1024)S(1)} %pad_clamp_fusion), kind=kCustom, calls=%fused_computation | custom fusion | bytes 526336 | tf_op jit(solution)/shard_map/jit(_take)/gather | solution.py:70
  52.2 1.6 collective-permute-start.4
  54.0 4.6 %collective-permute-done.4 = f32[128,512]{0,1:T(8,128)S(1)} collective-permute-done((f32[128,512]{0,1:T(8,128)S(1)}, f32[128,512]{0,1:T(8,128)S(1)}, u32[]{:S(2)}, u32[]{:S(2)}) %collective-permute-start.4) | collective-permute-done | bytes 262176 | tf_op jit(solution)/shard_map/ppermute | solution.py:72
  59.0 2.2 fusion.31
  61.3 4.3 %copy.39 = f32[128,4,1024]{2,1,0:T(4,128)} copy(f32[128,4,1024]{2,0,1:T(8,128)} %get-tuple-element.28) | data formatting | bytes 4194304
  65.5 1.5 collective-permute-start.5
  67.0 94.2 %all-reduce.5.cloned.1.call-done = f32[256,384]{0,1:T(8,128)} async-done(((f32[256,384]{0,1:T(8,128)}), f32[256,384]{0,1:T(8,128)}) %all-reduce.5.cloned.1.call-update) | async-done | bytes 393232 | tf_op jit(solution)/shard_map/psum | solution.py:84
  161.2 1.0 slice_add_fusion
  162.3 1.0 fusion.36
  163.3 11.7 %cholesky.50 = f32[128,128]{1,0:T(8,128)S(1)} custom-call(f32[128,128]{1,0:T(8,128)S(1)} %cholesky.118), custom_call_target="Cholesky" | custom-call | tf_op jit(solution)/shard_map/jit(cholesky)/cholesky | solution.py:87
  175.1 9.8 %custom-call.18 = f32[1,128,128]{1,2,0:T(8,128)S(1)} custom-call(f32[1,128,128]{2,1,0:T(8,128)S(1)} %get-tuple-element.37), custom_call_target="InvertDiagBlocksLowerTriangular" | custom-call | tf_op jit(solution)/shard_map/jit(cholesky)/cholesky | solution.py:87
  185.4 11.9 %cholesky.105 = f32[128,128]{1,0:T(8,128)S(1)} custom-call(f32[128,128]{1,0:T(8,128)S(1)} %convolution_subtract_fusion.2), custom_call_target="Cholesky" | custom-call | tf_op jit(solution)/shard_map/jit(cholesky)/cholesky | solution.py:87
  197.4 0.6 compare_reduce_fusion
  199.9 3.8 %while.1 = (s32[]{:T(128)}, f32[256,256]{1,0:T(8,128)S(1)}, s32[2,2]{1,0:T(2,128)S(1)}, f32[2,128,128]{2,1,0:T(8,128)S(1)}, s32[]{:T(128)}) while((s32[]{:T(128)}, f32[256,256]{1,0:T(8,128)S(1)}, s32[2,2]{1,0:T(2,128)S(1)}, f32[2,128,128]{2,1,0:T(8,128)S(1)}, s32[]{:T(128)}) %tuple.38), condition=%wide.while_cond, body=%wide.while_body.sunk | while | flops 2 | bytes 131181 | solution.py:88
  200.5 1.3 bitcast_dynamic-update-slice_fusion.2
  202.5 1.3 bitcast_dynamic-update-slice_fusion.2
  203.8 19.7 %custom-call.19 = f32[2,128,128]{1,2,0:T(8,128)S(1)} custom-call(f32[2,128,128]{2,1,0:T(8,128)S(1)} %get-tuple-element.9), custom_call_target="InvertDiagBlocksLowerTriangular" | custom-call | tf_op jit(solution)/shard_map/jit(_cho_solve)/triangular_solve | solution.py:88
  223.5 1.1 fusion.39
  224.6 1.1 convolution_subtract_fusion.1
  226.7 4.2 %fusion.30 = f32[128,4,1024]{2,0,1:T(8,128)S(1)} fusion(f32[128,4,1024]{2,0,1:T(8,128)S(1)} %get-tuple-element.29, f32[128,4,1024]{2,0,1:T(8,128)} %collective-permute-done.5, f32[128,128]{1,0:T(8,128)S(1)} %fusion.46, f32[128,128]{1,0:T(8,128)S(1)} %fusion.45), kind=kOutput, calls=%fused_computation.43 | convolution fusion | flops 1613266944 | bytes 6422528 | tf_op jit(solution)/shard_map/kj,kxy->jxy/dot_general | solution.py:90
  231.0 2.7 %copy.38 = f32[128,4,1024]{2,1,0:T(4,128)} copy(f32[128,4,1024]{2,0,1:T(8,128)S(1)} %fusion.30) | data formatting | bytes 4194304
  (55 shorter events, 5.2 us)
Async XLA Ops:
  7.2 6.8 %copy-start = (f32[8,4]{0,1:T(4,128)S(1)}, f32[8,4]{0,1:T(4,128)}, u32[]{:S(2)}) copy-start(f32[8,4]{0,1:T(4,128)} %param.11) | copy-start | bytes 388
  7.2 154.0 %all-reduce.5.cloned.1.call-start = ((), (), s32[]{:S(2)}) async-start(), calls=%async_computation | async-start | bytes 786432 | tf_op jit(solution)/shard_map/psum | solution.py:84
  7.2 6.8 %copy-start.4 = (s32[4,1024]{1,0:T(4,128)S(1)}, s32[4,1024]{1,0:T(4,128)}, u32[]{:S(2)}) copy-start(s32[4,1024]{1,0:T(4,128)} %param.10) | copy-start | bytes 49156
  10.1 8.5 %copy-start.2 = (f32[128,4,1024]{2,1,0:T(4,128)S(1)}, f32[128,4,1024]{2,1,0:T(4,128)}, u32[]{:S(2)}) copy-start(f32[128,4,1024]{2,1,0:T(4,128)} %param.8) | copy-start | bytes 6291460
  10.1 4.1 %collective-permute-start = (f32[128,1,1024]{2,0,1:T(8,128)S(1)}, f32[128,1,1024]{2,0,1:T(8,128)S(1)}, u32[]{:S(2)}, u32[]{:S(2)}) collective-permute-start(f32[128,1,1024]{2,0,1:T(8,128)S(1)} %get-tuple-element.32), channel_id=1, source_target_pairs={{0,1},{1,2},{2,3},{3,4},{4,5},{5,6},{6,7},{7,8},{8,9},{9,10},{10,1... | collective-permute-start | bytes 1572872 | tf_op jit(solution)/shard_map/ppermute | solution.py:19
  12.7 5.9 %collective-permute-start.1 = (f32[128,1,1024]{2,0,1:T(8,128)S(1)}, f32[128,1,1024]{2,0,1:T(8,128)S(1)}, u32[]{:S(2)}, u32[]{:S(2)}) collective-permute-start(f32[128,1,1024]{2,0,1:T(8,128)S(1)} %get-tuple-element.33), channel_id=1, source_target_pairs={{1,0},{2,1},{3,2},{4,3},{5,4},{6,5},{7,6},{8,7},{9,8},{10,9},{11,1... | collective-permute-start | bytes 1572872 | tf_op jit(solution)/shard_map/ppermute | solution.py:21
  21.2 13.2 %copy-start.1 = (f32[128,4,1024]{2,0,1:T(8,128)}, f32[128,4,1024]{2,0,1:T(8,128)S(1)}, u32[]{:S(2)}) copy-start(f32[128,4,1024]{2,0,1:T(8,128)S(1)} %fusion.8) | copy-start | bytes 6291460
  21.2 12.8 %copy-start.3 = (f32[128,512]{1,0:T(8,128)S(1)}, f32[128,512]{1,0:T(8,128)}, u32[]{:S(2)}) copy-start(f32[128,512]{1,0:T(8,128)} %param.15) | copy-start | bytes 786436
  21.2 12.9 %copy-start.7 = (s32[512]{0:T(512)S(1)}, s32[512]{0:T(512)}, u32[]{:S(2)}) copy-start(s32[512]{0:T(512)} %param.12) | copy-start | bytes 6148
  22.3 12.0 %collective-permute-start.2 = (f32[128,1,1024]{2,0,1:T(8,128)}, f32[128,1,1024]{2,0,1:T(8,128)S(1)}, u32[]{:S(2)}, u32[]{:S(2)}) collective-permute-start(f32[128,1,1024]{2,0,1:T(8,128)} %get-tuple-element.30), channel_id=1, source_target_pairs={{0,1},{1,2},{2,3},{3,4},{4,5},{5,6},{6,7},{7,8},{8,9},{9,10},{10,1... | collective-permute-start | bytes 1572872 | tf_op jit(solution)/shard_map/ppermute | solution.py:19
  32.6 6.1 %collective-permute-start.3 = (f32[128,1,1024]{2,0,1:T(8,128)}, f32[128,1,1024]{2,0,1:T(8,128)}, u32[]{:S(2)}, u32[]{:S(2)}) collective-permute-start(f32[128,1,1024]{2,0,1:T(8,128)} %get-tuple-element.31), channel_id=1, source_target_pairs={{1,0},{2,1},{3,2},{4,3},{5,4},{6,5},{7,6},{8,7},{9,8},{10,9},{11,1... | collective-permute-start | bytes 1572872 | tf_op jit(solution)/shard_map/ppermute | solution.py:21
  49.1 2.8 %copy-start.5 = (f32[512]{0:T(512)S(1)}, f32[512]{0:T(512)}, u32[]{:S(2)}) copy-start(f32[512]{0:T(512)} %param.14) | copy-start | bytes 6148
  49.1 2.8 %copy-start.6 = (f32[512]{0:T(512)S(1)}, f32[512]{0:T(512)}, u32[]{:S(2)}) copy-start(f32[512]{0:T(512)} %param.13) | copy-start | bytes 6148
  52.2 6.4 %collective-permute-start.4 = (f32[128,512]{0,1:T(8,128)S(1)}, f32[128,512]{0,1:T(8,128)S(1)}, u32[]{:S(2)}, u32[]{:S(2)}) collective-permute-start(f32[128,512]{0,1:T(8,128)S(1)} %get-tuple-element.23), channel_id=1, source_target_pairs={{0,16},{16,0},{1,17},{17,1},{2,18},{18,2},{3,19},{19,3},{4,20},{20... | collective-permute-start | bytes 786440 | tf_op jit(solution)/shard_map/ppermute | solution.py:72
  65.5 161.2 %collective-permute-start.5 = (f32[128,4,1024]{2,0,1:T(8,128)S(1)}, f32[128,4,1024]{2,0,1:T(8,128)}, u32[]{:S(2)}, u32[]{:S(2)}) collective-permute-start(f32[128,4,1024]{2,0,1:T(8,128)S(1)} %get-tuple-element.29), channel_id=1, source_target_pairs={{0,16},{16,0},{1,17},{17,1},{2,18},{18,2},{3,19},{19,3},{4,20},{20... | collective-permute-start | bytes 6291464 | tf_op jit(solution)/shard_map/ppermute | solution.py:85
Sparse Core Ops, SparseCore 0:
  61.4 99.7 all-reduce.4

commit v2 on v1

v2 whole, which is shorter than its diff:
```python
import functools
import math

import jax
import jax.numpy as jnp
from jax import lax
from jax.experimental import pallas as pl
from jax.experimental.pallas import tpu as pltpu
from jax.sharding import PartitionSpec as P

time_step = 0.06
MESH = pl.DeviceIdType.MESH
HIGHEST = lax.Precision.HIGHEST
HALO_PARTS = 4
PARAM_PARTS = 16
GROUP = 16


def forward_kernel(
    n, low, high, params, state, regime, regime_coefs, index, measured, spread, jitter,
    state_out, params_theirs_out, sums_out,
    mid, rates, coef, from_up, from_down, params_theirs, onehot, split, picked, own, theirs,
    stacked, part, landed, landed_high, total,
    halo_send, halo_recv, params_send, params_recv, field_send, field_recv, sum_send, sum_recv,
):
    members, cells = state.shape
    rows = regime.shape[0]
    columns = cells // rows
    me = lax.axis_index("space")
    up = lax.rem(me + n - 1, n)
    down = lax.rem(me + 1, n)
    twin = {"member": 1 - lax.axis_index("member")}
    bits = [lax.rem(lax.div(me, 1 << t), 2) for t in range(low + high)]
    pairs = [me + (1 - 2 * bits[t]) * (1 << t) for t in range(low + high)]

    barrier = pltpu.get_barrier_semaphore()
    greeted = [twin, {"space": up}, {"space": down}] + [{"space": q} for q in pairs]
    for device in greeted:
        pl.semaphore_signal(barrier, inc=1, device_id=device, device_id_type=MESH)
    pl.semaphore_wait(barrier, len(greeted))

    def send(src, dst, ssem, rsem, device):
        copy = pltpu.make_async_remote_copy(
            src_ref=src, dst_ref=dst, send_sem=ssem, recv_sem=rsem,
            device_id=device, device_id_type=MESH,
        )
        copy.start()
        return copy

    block = members // HALO_PARTS

    def halo(src, phase, c):
        span = pl.ds(c * block, block)
        return [
            send(src.at[span, pl.ds(cells - columns, columns)], from_up.at[phase, span],
                 halo_send.at[phase, 0, c], halo_recv.at[phase, 0, c], {"space": down}),
            send(src.at[span, pl.ds(0, columns)], from_down.at[phase, span],
                 halo_send.at[phase, 1, c], halo_recv.at[phase, 1, c], {"space": up}),
        ]

    params_rows = members // PARAM_PARTS
    params_copies = []

    def send_params(stop):
        for c in range(len(params_copies), stop):
            span = pl.ds(c * params_rows, params_rows)
            params_copies.append(send(params.at[span], params_theirs.at[span],
                                      params_send.at[c], params_recv.at[c], twin))

    first = [halo(state, 0, c) for c in range(HALO_PARTS)]
    send_params(6)

    for d in range(4):
        value = jnp.zeros(regime.shape, jnp.float32)
        for k in range(regime_coefs.shape[0]):
            value = jnp.where(regime[...] == k, regime_coefs[k, d], value)
        coef[d] = value

    observations = index.shape[1]
    local = index[...] - me * cells
    height = 256

    @pl.loop(0, cells // height)
    def _(b):
        start = pl.multiple_of(b * height, height)
        cell = lax.broadcasted_iota(jnp.int32, (height, observations), 0) + start
        onehot[pl.ds(start, height), :] = jnp.where(cell == local, 1.0, 0.0).astype(jnp.bfloat16)

    column = lax.broadcasted_iota(jnp.int32, (GROUP, columns), 1)

    def advance(src, phase, c):
        @pl.loop(0, block // GROUP)
        def _(g):
            start = pl.multiple_of(c * block + g * GROUP, GROUP)
            span = pl.ds(start, GROUP)
            for r in range(rows):
                here = pl.ds(r * columns, columns)
                x = src[span, here]
                if r > 0:
                    above = src[span, pl.ds((r - 1) * columns, columns)]
                else:
                    above = jnp.where(me > 0, from_up[phase, span, :], 0.0)
                if r < rows - 1:
                    below = src[span, pl.ds((r + 1) * columns, columns)]
                else:
                    below = jnp.where(me < n - 1, from_down[phase, span, :], 0.0)
                left = jnp.where(column == 0, 0.0, pltpu.roll(x, 1, 1))
                right = jnp.where(column == columns - 1, 0.0, pltpu.roll(x, columns - 1, 1))
                row = pl.ds(r, 1)
                flow = coef[0, row, :] * (above - x) + coef[1, row, :] * (below - x)
                flow = flow + coef[2, row, :] * (left - x) + coef[3, row, :] * (right - x)
                if phase == 0:
                    rate = time_step * jnp.exp(params[span, here])
                    rates[span, here] = rate
                    mid[span, here] = x + rate * flow
                else:
                    value = x + rates[span, here] * flow
                    state_out[span, here] = value
                    top = value.astype(jnp.bfloat16)
                    rest = value - top.astype(jnp.float32)
                    middle = rest.astype(jnp.bfloat16)
                    last = (rest - middle.astype(jnp.float32)).astype(jnp.bfloat16)
                    split[span, here] = top
                    split[pl.ds(start + members, GROUP), here] = middle
                    split[pl.ds(start + 2 * members, GROUP), here] = last

    second = []
    for c in range(HALO_PARTS):
        for copy in first[c]:
            copy.wait()
        advance(state, 0, c)
        second.append(halo(mid, 1, c))
        if c == 1:
            send_params(9)
    for c in range(HALO_PARTS):
        for copy in second[c]:
            copy.wait()
        advance(mid, 1, c)

    picked[...] = jnp.zeros_like(picked)
    depth = 1024

    @pl.loop(0, cells // depth)
    def _(b):
        span = pl.ds(pl.multiple_of(b * depth, depth), depth)
        picked[...] += jnp.dot(split[:, span], onehot[span, :], preferred_element_type=jnp.float32)

    own[...] = (picked[:members] + picked[members : 2 * members]) + picked[2 * members :]
    field = send(own, theirs, field_send, field_recv, twin)
    send_params(PARAM_PARTS)
    field.wait()

    everyone = 2 * members
    root = math.sqrt(everyone - 1)
    mean = (jnp.sum(own[...], axis=0, keepdims=True) + jnp.sum(theirs[...], axis=0, keepdims=True)) / everyone
    inverse = 1.0 / spread[...]
    scale = inverse / root
    stacked[:members] = (own[...] - mean) * scale
    stacked[members:everyone] = (theirs[...] - mean) * scale
    stacked[everyone:] = (measured[...] - own[...]) * inverse + jitter[...]
    contract = (((1,), (1,)), ((), ()))
    for h in range(2):
        part[h * members : (h + 1) * members] = lax.dot_general(
            stacked[h * members : (h + 1) * members], stacked[...], contract,
            precision=HIGHEST, preferred_element_type=jnp.float32,
        )

    start = 0
    size = everyone
    used = 0
    for t in range(low):
        size //= 2
        keep = pl.multiple_of(start + bits[t] * size, size)
        give = pl.multiple_of(start + (1 - bits[t]) * size, size)
        copy = send(part.at[pl.ds(give, size)], landed.at[pl.ds(used, size)],
                    sum_send.at[t], sum_recv.at[t], {"space": pairs[t]})
        copy.wait()
        part[pl.ds(keep, size)] = part[pl.ds(keep, size)] + landed[pl.ds(used, size)]
        used += size
        start = keep
    mine = pl.ds(start, size)
    for t in range(low, low + high):
        copy = send(part.at[mine], landed_high.at[t - low],
                    sum_send.at[t], sum_recv.at[t], {"space": pairs[t]})
        copy.wait()
        part[mine] = part[mine] + landed_high[t - low]
    total[mine] = part[mine]
    for t in reversed(range(low)):
        span = pl.ds(pl.multiple_of(start, size), size)
        slot = low + high + t
        copy = send(total.at[span], total.at[span],
                    sum_send.at[slot], sum_recv.at[slot], {"space": pairs[t]})
        copy.wait()
        start = start - bits[t] * size
        size *= 2
    sums_out[...] = total[...]
    for copy in params_copies:
        copy.wait()
    params_theirs_out[...] = params_theirs[...]


def solve_kernel(sums, params, params_theirs, out, work):
    everyone = sums.shape[0]
    members = everyone // 2
    width = sums.shape[1]
    r = lax.broadcasted_iota(jnp.int32, (everyone, width), 0)
    c = lax.broadcasted_iota(jnp.int32, (everyone, width), 1)
    work[...] = sums[...] + jnp.where(r == c, 1.0, 0.0)
    size = 32
    row = lax.broadcasted_iota(jnp.int32, (size, 2 * size), 0)
    lane = lax.broadcasted_iota(jnp.int32, (size, 2 * size), 1)
    unit = lax.broadcasted_iota(jnp.int32, (size, size), 0) == lax.broadcasted_iota(jnp.int32, (size, size), 1)
    for b in range(everyone // size):
        at = b * size
        pivot = work[at : at + size, at : at + size]
        aug = jnp.concatenate([pivot, jnp.where(unit, 1.0, 0.0)], axis=1)
        for k in range(size):
            line = aug[k : k + 1, :] / aug[k : k + 1, k : k + 1]
            aug = jnp.where(row == k, line, aug - aug[:, k : k + 1] * line)
        inverse = aug[:, size:]
        begin = (at + size) // 128 * 128
        lines = jnp.dot(inverse, work[at : at + size, begin:], precision=HIGHEST, preferred_element_type=jnp.float32)
        change = jnp.dot(work[:, at : at + size], lines, precision=HIGHEST, preferred_element_type=jnp.float32)
        work[:, begin:] = work[:, begin:] - change
        work[at : at + size, begin:] = lines
    mixing = work[:, everyone:] / math.sqrt(everyone - 1)
    weights = mixing.T
    tile = 512

    @pl.loop(0, params.shape[1] // tile)
    def _(b):
        span = pl.ds(pl.multiple_of(b * tile, tile), tile)
        out[:, span] = params[:, span] + (
            jnp.dot(weights[:, :members], params[:, span], precision=HIGHEST, preferred_element_type=jnp.float32)
            + jnp.dot(weights[:, members:], params_theirs[:, span], precision=HIGHEST, preferred_element_type=jnp.float32)
        )


def body(n, params, state, regime, regime_coefs, index, measured, spread, jitter):
    members, rows, columns = params.shape
    cells = rows * columns
    observations = index.shape[0]
    everyone = 2 * members
    levels = n.bit_length() - 1
    low = min(levels, 4)
    high = levels - low
    f32 = jnp.float32
    flat_params = params.reshape(members, cells)
    flat_state = state.reshape(members, cells)
    vmem = pl.BlockSpec(memory_space=pltpu.VMEM)
    smem = pl.BlockSpec(memory_space=pltpu.SMEM)
    width = everyone + members
    last = everyone >> low
    sems = pltpu.SemaphoreType.DMA
    flat_out, theirs, sums = pl.pallas_call(
        functools.partial(forward_kernel, n, low, high),
        out_shape=[
            jax.ShapeDtypeStruct((members, cells), f32),
            jax.ShapeDtypeStruct((members, cells), f32),
            jax.ShapeDtypeStruct((everyone, width), f32),
        ],
        in_specs=[vmem, vmem, vmem, smem, vmem, vmem, vmem, vmem],
        out_specs=[vmem, vmem, vmem],
        scratch_shapes=[
            pltpu.VMEM((members, cells), f32),
            pltpu.VMEM((members, cells), f32),
            pltpu.VMEM((4, rows, columns), f32),
            pltpu.VMEM((2, members, columns), f32),
            pltpu.VMEM((2, members, columns), f32),
            pltpu.VMEM((members, cells), f32),
            pltpu.VMEM((cells, observations), jnp.bfloat16),
            pltpu.VMEM((3 * members, cells), jnp.bfloat16),
            pltpu.VMEM((3 * members, observations), f32),
            pltpu.VMEM((members, observations), f32),
            pltpu.VMEM((members, observations), f32),
            pltpu.VMEM((3 * members, observations), f32),
            pltpu.VMEM((everyone, width), f32),
            pltpu.VMEM((everyone, width), f32),
            pltpu.VMEM((max(high, 1), last, width), f32),
            pltpu.VMEM((everyone, width), f32),
            sems((2, 2, HALO_PARTS)),
            sems((2, 2, HALO_PARTS)),
            sems((PARAM_PARTS,)),
            sems((PARAM_PARTS,)),
            sems,
            sems,
            sems((2 * low + high,)),
            sems((2 * low + high,)),
        ],
        compiler_params=pltpu.CompilerParams(
            collective_id=0, has_side_effects=True, vmem_limit_bytes=48 << 20
        ),
    )(flat_params, flat_state, regime, regime_coefs, index[None], measured[None], spread[None], jitter)
    revised = pl.pallas_call(
        solve_kernel,
        out_shape=jax.ShapeDtypeStruct((members, cells), f32),
        in_specs=[vmem, vmem, vmem],
        out_specs=vmem,
        scratch_shapes=[pltpu.VMEM((everyone, width), f32)],
        compiler_params=pltpu.CompilerParams(vmem_limit_bytes=32 << 20),
    )(sums, flat_params, theirs)
    return (revised.reshape(params.shape), flat_out.reshape(state.shape))


def solution(mesh):
    in_specs = (
        P("member", "space", None),
        P("member", "space", None),
        P("space", None),
        P(),
        P("space"),
        P("space"),
        P("space"),
        P("member", "space"),
    )
    out_specs = (P("member", "space", None), P("member", "space", None))
    return jax.shard_map(
        functools.partial(body, mesh.shape["space"]),
        mesh=mesh, in_specs=in_specs, out_specs=out_specs, check_vma=False,
    )
```

time: 241 us -> 117 us (0.49)
  waiting for transfers between devices: 108 us -> 0 us
  Pallas kernels: 0 us -> 100 us
  other arithmetic: 67.4 us -> 0 us
  starting transfers between devices: 18.5 us -> 0 us
  between operations: 15.6 us -> 0.7 us
  matrix products: 10.3 us -> 0 us
  local copies, waits for them, and re-layouts: 20.8 us -> 15.8 us
    pallas_call x0 -> x2, Pallas kernels: none -> 100 us  [the longest x1 68.3 us: body(): pl.pallas_call(functools.partial(forward_kernel, n, low, high), out_shape...]
    psum x1 -> x0, waiting for transfers between devices: 94.2 us -> none  [body(): rows = lax.psum(rows, 'space')]
    another operation x10 -> x0, other arithmetic: 54.5 us -> none  [the longest x7 34.8 us: body(): factor = jnp.linalg.cholesky(system)]
    ppermute x6 -> x0, starting transfers between devices: 18.5 us -> none  [the longest x2 12.9 us: with_halo(): lax.ppermute(tail, axis, [(i, (i + 1) % count) for i in range(ends)])]
    ppermute x6 -> x0, waiting for transfers between devices: 13.5 us -> none  [the longest x2 8.69 us: with_halo(): lax.ppermute(head, axis, [((i + 1) % count, i) for i in range(ends)])]
    add x3 -> x0, other arithmetic: 11 us -> none  [the longest x2 10 us: advance(): return center + rates * flow]
    dot_general x3 -> x0, matrix products: 6.63 us -> none  [the longest x1 4.25 us: body(): jnp.einsum('kj,kxy->jxy', mixing, piece, precision=lax.Precision.HIGHEST)]
    reshape x0 -> x2, local copies, waits for them, and re-layouts: none -> 6.04 us  [body(): return (revised.reshape(params.shape), flat_out.reshape(state.shape))]
  transfers between devices with their start and end apart: 7 -> 0, of which waited for: 5 -> 0; matrix products, arithmetic and copies ran while one was open for 29% -> 0% of each run, Pallas kernels for 0% -> 0%
where the time goes in v2:
time: 117 us
  Pallas kernels  100 us (85%)
  local copies, waits for them, and re-layouts  15.8 us (14%)
    pallas_call x1, Pallas kernels, body(): pl.pallas_call(functools.partial(forward_kernel, n, low, high), out_shape...  68.3 us
    pallas_call x1, Pallas kernels, body(): pl.pallas_call(solve_kernel, out_shape=jax.ShapeDtypeStruct((members, cel...  32 us
    unnamed x19, local copies, waits for them, and re-layouts  9.78 us
    reshape x2, local copies, waits for them, and re-layouts, body(): return (revised.reshape(params.shape), flat_out.reshape(state.shape))  6.04 us

profile of v2, /device:TPU:0, one launch (start us, length us, event | category | flops | bytes accessed | tf_op | source)
XLA Modules:
  0.0 116.8 jit_solution(592699313655931803)
XLA Ops:
  0.6 0.8 copy.10.regime_coefs
  1.4 0.0 copy-start.7
  1.4 4.7 %copy.11 = f32[16,8,4,1024]{3,1,2,0:T(8,128)} copy(f32[16,8,4,1024]{3,2,1,0:T(4,128)} %bitcast.13) | data formatting | bytes 4194304
  6.1 0.0 copy-done.7
  6.1 0.0 copy-start.2
  6.1 0.0 copy-start.3
  6.1 0.0 copy-start.4
  6.1 0.0 copy-start.5
  6.1 0.0 copy-start.6
  6.1 3.0 %copy.12 = f32[16,8,4,1024]{3,1,2,0:T(8,128)} copy(f32[16,8,4,1024]{3,2,1,0:T(4,128)S(1)} %bitcast.14) | data formatting | bytes 4194304
  9.1 0.0 copy-done.2
  9.1 0.0 copy-done.3
  9.1 0.0 copy-done.4
  9.1 0.0 copy-done.5
  9.1 0.0 copy-done.6
  9.1 0.0 copy-start
  9.1 68.3 %shard_map.95 = (f32[128,4096]{1,0:T(8,128)S(1)}, f32[128,4096]{1,0:T(8,128)S(1)}, f32[256,384]{1,0:T(8,128)S(1)}) custom-call(f32[128,4096]{1,0:T(8,128)} %bitcast.7, f32[128,4096]{1,0:T(8,128)} %bitcast.12, s32[4,1024]{1,0:T(4,128)S(1)} %copy-done.3, f32[8,4]{1,0:T(8,128)S(1)} %copy.10.regime_coefs, s32[1,512]{1,0:T(1,128)S(1)} %bitcast.9, ...), custom_call_target="tpu_custom_call" | custom-call | tf_op jit(solution)/shard_map/pallas_call | solution.py:255
  77.4 0.0 copy-start.1
  77.4 1.3 %copy-done.1 = f32[128,4096]{1,0:T(8,128)} copy-done((f32[128,4096]{1,0:T(8,128)}, f32[128,4096]{1,0:T(8,128)S(1)}, u32[]{:S(2)}) %copy-start.1) | copy-done | bytes 2097176
  78.7 0.0 copy-done
  78.7 32.0 %shard_map.96 = f32[128,4096]{1,0:T(8,128)S(1)} custom-call(f32[256,384]{1,0:T(8,128)S(1)} %get-tuple-element.5.sums, f32[128,4096]{1,0:T(8,128)S(1)} %bitcast.8, f32[128,4096]{1,0:T(8,128)S(1)} %get-tuple-element.6.params_theirs), custom_call_target="tpu_custom_call" | custom-call | tf_op jit(solution)/shard_map/pallas_call | solution.py:294
  110.8 2.4 %reshape.18 = f32[128,4,1024]{2,1,0:T(4,128)} reshape(f32[128,4096]{1,0:T(8,128)S(1)} %shard_map.96) | data formatting | bytes 4194304 | tf_op jit(solution)/shard_map/reshape | solution.py:302
  113.2 3.6 %reshape.19 = f32[128,4,1024]{2,1,0:T(4,128)} reshape(f32[128,4096]{1,0:T(8,128)} %copy-done.1) | data formatting | bytes 4194304 | tf_op jit(solution)/shard_map/reshape | solution.py:302
Async XLA Ops:
  1.4 4.7 %copy-start.7 = (f32[128,4,1024]{2,1,0:T(4,128)S(1)}, f32[128,4,1024]{2,1,0:T(4,128)}, u32[]{:S(2)}) copy-start(f32[128,4,1024]{2,1,0:T(4,128)} %param.9) | copy-start | bytes 6291460
  6.1 3.0 %copy-start.2 = (f32[128,512]{1,0:T(8,128)S(1)}, f32[128,512]{1,0:T(8,128)}, u32[]{:S(2)}) copy-start(f32[128,512]{1,0:T(8,128)} %jitter.1) | copy-start | bytes 786436
  6.1 3.0 %copy-start.3 = (s32[4,1024]{1,0:T(4,128)S(1)}, s32[4,1024]{1,0:T(4,128)}, u32[]{:S(2)}) copy-start(s32[4,1024]{1,0:T(4,128)} %regime.1) | copy-start | bytes 49156
  6.1 3.0 %copy-start.4 = (s32[512]{0:T(512)S(1)}, s32[512]{0:T(512)}, u32[]{:S(2)}) copy-start(s32[512]{0:T(512)} %param.12) | copy-start | bytes 6148
  6.1 3.0 %copy-start.5 = (f32[512]{0:T(512)S(1)}, f32[512]{0:T(512)}, u32[]{:S(2)}) copy-start(f32[512]{0:T(512)} %param.13) | copy-start | bytes 6148
  6.1 3.0 %copy-start.6 = (f32[512]{0:T(512)S(1)}, f32[512]{0:T(512)}, u32[]{:S(2)}) copy-start(f32[512]{0:T(512)} %param.14) | copy-start | bytes 6148
  9.1 69.6 %copy-start = (f32[16,8,4,1024]{3,1,2,0:T(8,128)S(1)}, f32[16,8,4,1024]{3,1,2,0:T(8,128)}, u32[]{:S(2)}) copy-start(f32[16,8,4,1024]{3,1,2,0:T(8,128)} %copy.11) | copy-start | bytes 6291460
  77.4 1.3 %copy-start.1 = (f32[128,4096]{1,0:T(8,128)}, f32[128,4096]{1,0:T(8,128)S(1)}, u32[]{:S(2)}) copy-start(f32[128,4096]{1,0:T(8,128)S(1)} %get-tuple-element.7) | copy-start | bytes 6291460

commit v3 on v2

--- a/solution.py
+++ b/solution.py
@@ -17,13 +17,13 @@
 
 
 def forward_kernel(
-    n, low, high, params, state, regime, regime_coefs, index, measured, spread, jitter,
-    state_out, params_theirs_out, sums_out,
-    mid, rates, coef, from_up, from_down, params_theirs, onehot, split, picked, own, theirs,
+    n, low, high, params_hbm, state_hbm, regime, regime_coefs, index, measured, spread, jitter,
+    state_out, theirs_out, sums_out,
+    params, state, result, mid, rates, coef, from_up, from_down, onehot, split, picked, own, theirs,
     stacked, part, landed, landed_high, total,
-    halo_send, halo_recv, params_send, params_recv, field_send, field_recv, sum_send, sum_recv,
+    halo_send, halo_recv, params_send, params_recv, field_send, field_recv, sum_send, sum_recv, load_sem, store_sem,
 ):
-    members, cells = state.shape
+    members, cells = params.shape
     rows = regime.shape[0]
     columns = cells // rows
     me = lax.axis_index("space")
@@ -33,6 +33,18 @@
     bits = [lax.rem(lax.div(me, 1 << t), 2) for t in range(low + high)]
     pairs = [me + (1 - 2 * bits[t]) * (1 << t) for t in range(low + high)]
 
+    def rowwise(flat, whole, sem, outward):
+        copies = []
+        for r in range(rows):
+            pair = (flat.at[:, pl.ds(r * columns, columns)], whole.at[:, r, :])
+            src, dst = pair if outward else pair[::-1]
+            copies.append(pltpu.make_async_copy(src, dst, sem.at[r]))
+            copies[-1].start()
+        return copies
+
+    params_loads = rowwise(params, params_hbm, load_sem.at[0], False)
+    state_loads = rowwise(state, state_hbm, load_sem.at[1], False)
+
     barrier = pltpu.get_barrier_semaphore()
     greeted = [twin, {"space": up}, {"space": down}] + [{"space": q} for q in pairs]
     for device in greeted:
@@ -51,10 +63,14 @@
 
     def halo(src, phase, c):
         span = pl.ds(c * block, block)
+        if phase == 0:
+            bottom, top = src.at[span, rows - 1, :], src.at[span, 0, :]
+        else:
+            bottom, top = src.at[span, pl.ds(cells - columns, columns)], src.at[span, pl.ds(0, columns)]
         return [
-            send(src.at[span, pl.ds(cells - columns, columns)], from_up.at[phase, span],
+            send(bottom, from_up.at[phase, span],
                  halo_send.at[phase, 0, c], halo_recv.at[phase, 0, c], {"space": down}),
-            send(src.at[span, pl.ds(0, columns)], from_down.at[phase, span],
+            send(top, from_down.at[phase, span],
                  halo_send.at[phase, 1, c], halo_recv.at[phase, 1, c], {"space": up}),
         ]
 
@@ -64,10 +80,10 @@
     def send_params(stop):
         for c in range(len(params_copies), stop):
             span = pl.ds(c * params_rows, params_rows)
-            params_copies.append(send(params.at[span], params_theirs.at[span],
+            params_copies.append(send(params_hbm.at[span], theirs_out.at[span],
                                       params_send.at[c], params_recv.at[c], twin))
 
-    first = [halo(state, 0, c) for c in range(HALO_PARTS)]
+    first = [halo(state_hbm, 0, c) for c in range(HALO_PARTS)]
     send_params(6)
 
     for d in range(4):
@@ -115,7 +131,7 @@
                     mid[span, here] = x + rate * flow
                 else:
                     value = x + rates[span, here] * flow
-                    state_out[span, here] = value
+                    result[span, here] = value
                     top = value.astype(jnp.bfloat16)
                     rest = value - top.astype(jnp.float32)
                     middle = rest.astype(jnp.bfloat16)
@@ -124,6 +140,8 @@
                     split[pl.ds(start + members, GROUP), here] = middle
                     split[pl.ds(start + 2 * members, GROUP), here] = last
 
+    for copy in params_loads + state_loads:
+        copy.wait()
     second = []
     for c in range(HALO_PARTS):
         for copy in first[c]:
@@ -137,6 +155,7 @@
             copy.wait()
         advance(mid, 1, c)
 
+    state_stores = rowwise(result, state_out, store_sem, True)
     picked[...] = jnp.zeros_like(picked)
     depth = 1024
 
@@ -194,12 +213,18 @@
         start = start - bits[t] * size
         size *= 2
     sums_out[...] = total[...]
-    for copy in params_copies:
-        copy.wait()
-    params_theirs_out[...] = params_theirs[...]
-
-
-def solve_kernel(sums, params, params_theirs, out, work):
+    for copy in params_copies + state_stores:
+        copy.wait()
+
+
+def solve_kernel(sums, params_hbm, theirs_hbm, out_hbm, work, params, params_theirs, out, sem):
+    rows, columns = params_hbm.shape[1:]
+    loads = []
+    for whole, flat, i in ((params_hbm, params, 0), (theirs_hbm, params_theirs, 1)):
+        for r in range(rows):
+            loads.append(pltpu.make_async_copy(
+                whole.at[:, r, :], flat.at[:, pl.ds(r * columns, columns)], sem.at[i, r]))
+            loads[-1].start()
     everyone = sums.shape[0]
     members = everyone // 2
     width = sums.shape[1]
@@ -226,14 +251,22 @@
     mixing = work[:, everyone:] / math.sqrt(everyone - 1)
     weights = mixing.T
     tile = 512
-
-    @pl.loop(0, params.shape[1] // tile)
-    def _(b):
-        span = pl.ds(pl.multiple_of(b * tile, tile), tile)
-        out[:, span] = params[:, span] + (
-            jnp.dot(weights[:, :members], params[:, span], precision=HIGHEST, preferred_element_type=jnp.float32)
-            + jnp.dot(weights[:, members:], params_theirs[:, span], precision=HIGHEST, preferred_element_type=jnp.float32)
-        )
+    for copy in loads:
+        copy.wait()
+    stores = []
+    for r in range(rows):
+        @pl.loop(0, columns // tile)
+        def _(b):
+            span = pl.ds(pl.multiple_of(r * columns + b * tile, tile), tile)
+            out[:, span] = params[:, span] + (
+                jnp.dot(weights[:, :members], params[:, span], precision=HIGHEST, preferred_element_type=jnp.float32)
+                + jnp.dot(weights[:, members:], params_theirs[:, span], precision=HIGHEST, preferred_element_type=jnp.float32)
+            )
+        stores.append(pltpu.make_async_copy(
+            out.at[:, pl.ds(r * columns, columns)], out_hbm.at[:, r, :], sem.at[2, r]))
+        stores[-1].start()
+    for copy in stores:
+        copy.wait()
 
 
 def body(n, params, state, regime, regime_coefs, index, measured, spread, jitter):
@@ -245,29 +278,31 @@
     low = min(levels, 4)
     high = levels - low
     f32 = jnp.float32
-    flat_params = params.reshape(members, cells)
-    flat_state = state.reshape(members, cells)
+    anywhere = pl.BlockSpec(memory_space=pl.ANY)
+    flat = pltpu.VMEM((members, cells), f32)
     vmem = pl.BlockSpec(memory_space=pltpu.VMEM)
     smem = pl.BlockSpec(memory_space=pltpu.SMEM)
     width = everyone + members
     last = everyone >> low
     sems = pltpu.SemaphoreType.DMA
-    flat_out, theirs, sums = pl.pallas_call(
+    state_out, theirs, sums = pl.pallas_call(
         functools.partial(forward_kernel, n, low, high),
         out_shape=[
-            jax.ShapeDtypeStruct((members, cells), f32),
-            jax.ShapeDtypeStruct((members, cells), f32),
+            jax.ShapeDtypeStruct(state.shape, f32),
+            jax.ShapeDtypeStruct(params.shape, f32),
             jax.ShapeDtypeStruct((everyone, width), f32),
         ],
-        in_specs=[vmem, vmem, vmem, smem, vmem, vmem, vmem, vmem],
-        out_specs=[vmem, vmem, vmem],
+        in_specs=[anywhere, anywhere, vmem, smem, vmem, vmem, vmem, vmem],
+        out_specs=[anywhere, anywhere, vmem],
         scratch_shapes=[
-            pltpu.VMEM((members, cells), f32),
-            pltpu.VMEM((members, cells), f32),
+            flat,
+            flat,
+            flat,
+            flat,
+            flat,
             pltpu.VMEM((4, rows, columns), f32),
             pltpu.VMEM((2, members, columns), f32),
             pltpu.VMEM((2, members, columns), f32),
-            pltpu.VMEM((members, cells), f32),
             pltpu.VMEM((cells, observations), jnp.bfloat16),
             pltpu.VMEM((3 * members, cells), jnp.bfloat16),
             pltpu.VMEM((3 * members, observations), f32),
@@ -286,20 +321,22 @@
             sems,
             sems((2 * low + high,)),
             sems((2 * low + high,)),
+            sems((2, rows)),
+            sems((rows,)),
         ],
         compiler_params=pltpu.CompilerParams(
             collective_id=0, has_side_effects=True, vmem_limit_bytes=48 << 20
         ),
-    )(flat_params, flat_state, regime, regime_coefs, index[None], measured[None], spread[None], jitter)
+    )(params, state, regime, regime_coefs, index[None], measured[None], spread[None], jitter)
     revised = pl.pallas_call(
         solve_kernel,
-        out_shape=jax.ShapeDtypeStruct((members, cells), f32),
-        in_specs=[vmem, vmem, vmem],
-        out_specs=vmem,
-        scratch_shapes=[pltpu.VMEM((everyone, width), f32)],
+        out_shape=jax.ShapeDtypeStruct(params.shape, f32),
+        in_specs=[vmem, anywhere, anywhere],
+        out_specs=anywhere,
+        scratch_shapes=[pltpu.VMEM((everyone, width), f32), flat, flat, flat, sems((3, rows))],
         compiler_params=pltpu.CompilerParams(vmem_limit_bytes=32 << 20),
-    )(sums, flat_params, theirs)
-    return (revised.reshape(params.shape), flat_out.reshape(state.shape))
+    )(sums, params, theirs)
+    return (revised, state_out)
 
 
 def solution(mesh):

time: 117 us -> 111 us (0.949)
  local copies, waits for them, and re-layouts: 15.8 us -> 5.79 us
  Pallas kernels: 100 us -> 104 us
    reshape x2 -> x0, local copies, waits for them, and re-layouts: 6.04 us -> none  [body(): return (revised.reshape(params.shape), flat_out.reshape(state.shape))]
    unnamed x19 -> x14, local copies, waits for them, and re-layouts: 9.78 us -> 5.79 us
    pallas_call x1, Pallas kernels: 32 us -> 35.8 us  [body(): pl.pallas_call(solve_kernel, out_shape=jax.ShapeDtypeStruct(params.shape,...]
where the time goes in v3:
time: 111 us
  Pallas kernels  104 us (94%)
  local copies, waits for them, and re-layouts  5.79 us (5%)
    pallas_call x1, Pallas kernels, body(): pl.pallas_call(functools.partial(forward_kernel, n, low, high), out_shape...  68.4 us
    pallas_call x1, Pallas kernels, body(): pl.pallas_call(solve_kernel, out_shape=jax.ShapeDtypeStruct(params.shape,...  35.8 us
    unnamed x14, local copies, waits for them, and re-layouts  5.79 us

profile of v3, /device:TPU:0, one launch (start us, length us, event | category | flops | bytes accessed | tf_op | source)
XLA Modules:
  0.0 110.6 jit_solution(4564390029001067715)
XLA Ops:
  0.6 0.8 copy.10.regime_coefs
  1.4 0.0 copy-start.1
  1.4 0.9 copy-done.1
  2.3 0.0 copy-start.2
  2.3 0.7 copy-done.2
  3.1 0.0 copy-start.3
  3.1 0.7 copy-done.3
  3.7 0.0 copy-start.4
  3.7 0.7 copy-done.4
  4.4 0.0 copy-start.5
  4.4 0.7 copy-done.5
  5.1 0.0 copy-start
  5.1 68.4 %shard_map.95 = (f32[128,4,1024]{2,1,0:T(4,128)S(1)}, f32[128,4,1024]{2,1,0:T(4,128)S(1)}, f32[256,384]{1,0:T(8,128)S(1)}) custom-call(f32[128,4,1024]{2,1,0:T(4,128)} %params_hbm.3, f32[128,4,1024]{2,1,0:T(4,128)} %state_hbm.1, s32[4,1024]{1,0:T(4,128)S(1)} %copy-done.2, f32[8,4]{1,0:T(8,128)S(1)} %copy.10.regime_coefs, s32[1,512]{1,0:T(1,128)S(1)} %bitcast.3, ...), custom_call_target="tpu_custom_call" | custom-call | tf_op jit(solution)/shard_map/pallas_call | solution.py:288
  73.5 0.0 copy-done
  73.5 35.8 %shard_map.96 = f32[128,4,1024]{2,1,0:T(4,128)} custom-call(f32[256,384]{1,0:T(8,128)S(1)} %get-tuple-element.5.sums, f32[128,4,1024]{2,1,0:T(4,128)S(1)} %copy-done, f32[128,4,1024]{2,1,0:T(4,128)S(1)} %get-tuple-element.6.theirs_hbm), custom_call_target="tpu_custom_call" | custom-call | tf_op jit(solution)/shard_map/pallas_call | solution.py:331
  109.3 1.3 %copy.12 = f32[128,4,1024]{2,1,0:T(4,128)} copy(f32[128,4,1024]{2,1,0:T(4,128)S(1)} %get-tuple-element.11) | data formatting | bytes 4194304
Async XLA Ops:
  1.4 0.9 copy-start.1
  2.3 0.7 copy-start.2
  3.1 0.7 copy-start.3
  3.7 0.7 copy-start.4
  4.4 0.7 copy-start.5
  5.1 68.4 %copy-start = (f32[128,4,1024]{2,1,0:T(4,128)S(1)}, f32[128,4,1024]{2,1,0:T(4,128)}, u32[]{:S(2)}) copy-start(f32[128,4,1024]{2,1,0:T(4,128)} %params_hbm.3) | copy-start | bytes 6291460

commit v4 on v3

--- a/solution.py
+++ b/solution.py
@@ -231,7 +231,7 @@
     r = lax.broadcasted_iota(jnp.int32, (everyone, width), 0)
     c = lax.broadcasted_iota(jnp.int32, (everyone, width), 1)
     work[...] = sums[...] + jnp.where(r == c, 1.0, 0.0)
-    size = 32
+    size = 64
     row = lax.broadcasted_iota(jnp.int32, (size, 2 * size), 0)
     lane = lax.broadcasted_iota(jnp.int32, (size, 2 * size), 1)
     unit = lax.broadcasted_iota(jnp.int32, (size, size), 0) == lax.broadcasted_iota(jnp.int32, (size, size), 1)
@@ -239,9 +239,17 @@
         at = b * size
         pivot = work[at : at + size, at : at + size]
         aug = jnp.concatenate([pivot, jnp.where(unit, 1.0, 0.0)], axis=1)
-        for k in range(size):
-            line = aug[k : k + 1, :] / aug[k : k + 1, k : k + 1]
-            aug = jnp.where(row == k, line, aug - aug[:, k : k + 1] * line)
+        for k in range(0, size, 2):
+            col0 = jnp.broadcast_to(aug[:, k : k + 1], aug.shape)
+            col1 = jnp.broadcast_to(aug[:, k + 1 : k + 2], aug.shape)
+            p00, p01 = col0[k : k + 1, :], col1[k : k + 1, :]
+            p11 = col1[k + 1 : k + 2, :]
+            scale = 1.0 / (p00 * p11 - p01 * p01)
+            row0, row1 = aug[k : k + 1, :], aug[k + 1 : k + 2, :]
+            line0 = (p11 * row0 - p01 * row1) * scale
+            line1 = (p00 * row1 - p01 * row0) * scale
+            aug = aug - col0 * line0 - col1 * line1
+            aug = jnp.where(row == k, line0, jnp.where(row == k + 1, line1, aug))
         inverse = aug[:, size:]
         begin = (at + size) // 128 * 128
         lines = jnp.dot(inverse, work[at : at + size, begin:], precision=HIGHEST, preferred_element_type=jnp.float32)
@@ -250,6 +258,8 @@
         work[at : at + size, begin:] = lines
     mixing = work[:, everyone:] / math.sqrt(everyone - 1)
     weights = mixing.T
+    heavy = weights.astype(jnp.bfloat16)
+    light = (weights - heavy.astype(jnp.float32)).astype(jnp.bfloat16)
     tile = 512
     for copy in loads:
         copy.wait()
@@ -258,10 +268,13 @@
         @pl.loop(0, columns // tile)
         def _(b):
             span = pl.ds(pl.multiple_of(r * columns + b * tile, tile), tile)
-            out[:, span] = params[:, span] + (
-                jnp.dot(weights[:, :members], params[:, span], precision=HIGHEST, preferred_element_type=jnp.float32)
-                + jnp.dot(weights[:, members:], params_theirs[:, span], precision=HIGHEST, preferred_element_type=jnp.float32)
-            )
+            piece = jnp.concatenate([params[:, span], params_theirs[:, span]], axis=0)
+            top = piece.astype(jnp.bfloat16)
+            rest = (piece - top.astype(jnp.float32)).astype(jnp.bfloat16)
+            update = jnp.dot(heavy, top, preferred_element_type=jnp.float32)
+            update += jnp.dot(heavy, rest, preferred_element_type=jnp.float32)
+            update += jnp.dot(light, top, preferred_element_type=jnp.float32)
+            out[:, span] = params[:, span] + update
         stores.append(pltpu.make_async_copy(
             out.at[:, pl.ds(r * columns, columns)], out_hbm.at[:, r, :], sem.at[2, r]))
         stores[-1].start()

time: 111 us -> 96.7 us (0.87)
  Pallas kernels: 104 us -> 89.9 us
    pallas_call x1, Pallas kernels: 35.8 us -> 21.5 us  [body(): pl.pallas_call(solve_kernel, out_shape=jax.ShapeDtypeStruct(params.shape,...]
where the time goes in v4:
time: 96.7 us; the launch traced here: 96.4 us
  Pallas kernels  89.9 us (93%)
  local copies, waits for them, and re-layouts  5.79 us (6%)
    pallas_call x1, Pallas kernels, body(): pl.pallas_call(functools.partial(forward_kernel, n, low, high), out_shape...  68.4 us
    pallas_call x1, Pallas kernels, body(): pl.pallas_call(solve_kernel, out_shape=jax.ShapeDtypeStruct(params.shape,...  21.5 us
    unnamed x14, local copies, waits for them, and re-layouts  5.79 us

profile of v4, /device:TPU:0, one launch (start us, length us, event | category | flops | bytes accessed | tf_op | source)
XLA Modules:
  0.0 96.4 jit_solution(15150536515737517363)
XLA Ops:
  0.6 0.8 copy.10.regime_coefs
  1.4 0.0 copy-start.1
  1.4 0.9 copy-done.1
  2.3 0.0 copy-start.2
  2.3 0.7 copy-done.2
  3.1 0.0 copy-start.3
  3.1 0.7 copy-done.3
  3.7 0.0 copy-start.4
  3.7 0.7 copy-done.4
  4.4 0.0 copy-start.5
  4.4 0.7 copy-done.5
  5.1 0.0 copy-start
  5.1 68.4 %shard_map.95 = (f32[128,4,1024]{2,1,0:T(4,128)S(1)}, f32[128,4,1024]{2,1,0:T(4,128)S(1)}, f32[256,384]{1,0:T(8,128)S(1)}) custom-call(f32[128,4,1024]{2,1,0:T(4,128)} %params_hbm.3, f32[128,4,1024]{2,1,0:T(4,128)} %state_hbm.1, s32[4,1024]{1,0:T(4,128)S(1)} %copy-done.2, f32[8,4]{1,0:T(8,128)S(1)} %copy.10.regime_coefs, s32[1,512]{1,0:T(1,128)S(1)} %bitcast.3, ...), custom_call_target="tpu_custom_call" | custom-call | tf_op jit(solution)/shard_map/pallas_call | solution.py:301
  73.5 0.0 copy-done
  73.5 21.5 %shard_map.96 = f32[128,4,1024]{2,1,0:T(4,128)} custom-call(f32[256,384]{1,0:T(8,128)S(1)} %get-tuple-element.5.sums, f32[128,4,1024]{2,1,0:T(4,128)S(1)} %copy-done, f32[128,4,1024]{2,1,0:T(4,128)S(1)} %get-tuple-element.6.theirs_hbm), custom_call_target="tpu_custom_call" | custom-call | tf_op jit(solution)/shard_map/pallas_call | solution.py:344
  95.1 1.3 %copy.12 = f32[128,4,1024]{2,1,0:T(4,128)} copy(f32[128,4,1024]{2,1,0:T(4,128)S(1)} %get-tuple-element.11) | data formatting | bytes 4194304
Async XLA Ops:
  1.4 0.9 copy-start.1
  2.3 0.7 copy-start.2
  3.1 0.7 copy-start.3
  3.7 0.7 copy-start.4
  4.4 0.7 copy-start.5
  5.1 68.4 %copy-start = (f32[128,4,1024]{2,1,0:T(4,128)S(1)}, f32[128,4,1024]{2,1,0:T(4,128)}, u32[]{:S(2)}) copy-start(f32[128,4,1024]{2,1,0:T(4,128)} %params_hbm.3) | copy-start | bytes 6291460

commit v5 on v4

--- a/solution.py
+++ b/solution.py
@@ -17,11 +17,12 @@
 
 
 def forward_kernel(
-    n, low, high, params_hbm, state_hbm, regime, regime_coefs, index, measured, spread, jitter,
+    n, low, high, params_hbm, state_hbm, regime_hbm, regime_coefs, index_hbm, measured_hbm, spread_hbm, jitter_hbm,
     state_out, theirs_out, sums_out,
     params, state, result, mid, rates, coef, from_up, from_down, onehot, split, picked, own, theirs,
     stacked, part, landed, landed_high, total,
     halo_send, halo_recv, params_send, params_recv, field_send, field_recv, sum_send, sum_recv, load_sem, store_sem,
+    regime, index, measured, spread, jitter, small_sem,
 ):
     members, cells = params.shape
     rows = regime.shape[0]
@@ -42,6 +43,12 @@
             copies[-1].start()
         return copies
 
+    small_loads = []
+    for i, (src, dst) in enumerate([
+        (regime_hbm, regime), (index_hbm, index), (measured_hbm, measured), (spread_hbm, spread), (jitter_hbm, jitter),
+    ]):
+        small_loads.append(pltpu.make_async_copy(src, dst, small_sem.at[i]))
+        small_loads[-1].start()
     params_loads = rowwise(params, params_hbm, load_sem.at[0], False)
     state_loads = rowwise(state, state_hbm, load_sem.at[1], False)
 
@@ -86,6 +93,8 @@
     first = [halo(state_hbm, 0, c) for c in range(HALO_PARTS)]
     send_params(6)
 
+    for copy in small_loads:
+        copy.wait()
     for d in range(4):
         value = jnp.zeros(regime.shape, jnp.float32)
         for k in range(regime_coefs.shape[0]):
@@ -292,6 +301,7 @@
     high = levels - low
     f32 = jnp.float32
     anywhere = pl.BlockSpec(memory_space=pl.ANY)
+    hbm = pl.BlockSpec(memory_space=pltpu.HBM)
     flat = pltpu.VMEM((members, cells), f32)
     vmem = pl.BlockSpec(memory_space=pltpu.VMEM)
     smem = pl.BlockSpec(memory_space=pltpu.SMEM)
@@ -305,7 +315,7 @@
             jax.ShapeDtypeStruct(params.shape, f32),
             jax.ShapeDtypeStruct((everyone, width), f32),
         ],
-        in_specs=[anywhere, anywhere, vmem, smem, vmem, vmem, vmem, vmem],
+        in_specs=[anywhere, anywhere, hbm, smem, hbm, hbm, hbm, hbm],
         out_specs=[anywhere, anywhere, vmem],
         scratch_shapes=[
             flat,
@@ -336,9 +346,15 @@
             sems((2 * low + high,)),
             sems((2, rows)),
             sems((rows,)),
+            pltpu.VMEM(regime.shape, jnp.int32),
+            pltpu.VMEM((1, observations), jnp.int32),
+            pltpu.VMEM((1, observations), f32),
+            pltpu.VMEM((1, observations), f32),
+            pltpu.VMEM(jitter.shape, f32),
+            sems((5,)),
         ],
         compiler_params=pltpu.CompilerParams(
-            collective_id=0, has_side_effects=True, vmem_limit_bytes=48 << 20
+            collective_id=0, has_side_effects=True, vmem_limit_bytes=62 << 20
         ),
     )(params, state, regime, regime_coefs, index[None], measured[None], spread[None], jitter)
     revised = pl.pallas_call(

time: 96.7 us -> 97.1 us (level)
  local copies, waits for them, and re-layouts: 5.79 us -> 6.85 us
    unnamed x14 -> x10, local copies, waits for them, and re-layouts: 5.79 us -> 6.85 us
where the time goes in v5:
time: 97.1 us; the launch traced here: 96.8 us
  Pallas kernels  89.3 us (92%)
  local copies, waits for them, and re-layouts  6.85 us (7%)
    pallas_call x1, Pallas kernels, body(): pl.pallas_call(functools.partial(forward_kernel, n, low, high), out_shape...  67.8 us
    pallas_call x1, Pallas kernels, body(): pl.pallas_call(solve_kernel, out_shape=jax.ShapeDtypeStruct(params.shape,...  21.5 us
    unnamed x10, local copies, waits for them, and re-layouts  6.85 us

profile of v5, /device:TPU:0, one launch (start us, length us, event | category | flops | bytes accessed | tf_op | source)
XLA Modules:
  0.0 96.8 jit_solution(15343938640073671928)
XLA Ops:
  0.6 1.3 %copy.10.regime_coefs = f32[8,4]{1,0:T(8,128)} copy(f32[8,4]{0,1:T(4,128)} %param.11) | data formatting | bytes 256 | tf_op args[3]
  2.0 67.8 %shard_map.95 = (f32[128,4,1024]{2,1,0:T(4,128)}, f32[128,4,1024]{2,1,0:T(4,128)}, f32[256,384]{1,0:T(8,128)}) custom-call(f32[128,4,1024]{2,1,0:T(4,128)} %params_hbm.3, f32[128,4,1024]{2,1,0:T(4,128)} %state_hbm.1, s32[4,1024]{1,0:T(4,128)} %regime_hbm.1, f32[8,4]{1,0:T(8,128)} %copy.10.regime_coefs, s32[1,512]{1,0:T(1,128)} %bitcast.3, f32[1,512]{1,0:T(1,128)} %bitcast.4, ...), custom_call_target="tpu_custom_call" | custom-call | tf_op jit(solution)/shard_map/pallas_call | solution.py:311
  69.8 0.0 copy-start
  69.8 1.6 %copy-done = f32[128,4,1024]{2,1,0:T(4,128)S(1)} copy-done((f32[128,4,1024]{2,1,0:T(4,128)S(1)}, f32[128,4,1024]{2,1,0:T(4,128)}, u32[]{:S(2)}) %copy-start) | copy-done | bytes 2097176
  71.4 0.0 copy-start.1
  71.4 1.6 %copy-done.1 = f32[128,4,1024]{2,1,0:T(4,128)S(1)} copy-done((f32[128,4,1024]{2,1,0:T(4,128)S(1)}, f32[128,4,1024]{2,1,0:T(4,128)}, u32[]{:S(2)}) %copy-start.1) | copy-done | bytes 2097176
  73.0 0.0 copy-start.2
  73.0 1.0 %copy-done.2 = f32[256,384]{1,0:T(8,128)S(1)} copy-done((f32[256,384]{1,0:T(8,128)S(1)}, f32[256,384]{1,0:T(8,128)}, u32[]{:S(2)}) %copy-start.2) | copy-done | bytes 393240
  74.0 0.0 copy-start.3
  74.0 21.5 %shard_map.96 = f32[128,4,1024]{2,1,0:T(4,128)} custom-call(f32[256,384]{1,0:T(8,128)S(1)} %copy-done.2, f32[128,4,1024]{2,1,0:T(4,128)S(1)} %copy-done, f32[128,4,1024]{2,1,0:T(4,128)S(1)} %copy-done.1), custom_call_target="tpu_custom_call" | custom-call | tf_op jit(solution)/shard_map/pallas_call | solution.py:360
  95.5 0.0 copy-done.3
  95.5 1.3 %copy.12 = f32[128,4,1024]{2,1,0:T(4,128)} copy(f32[128,4,1024]{2,1,0:T(4,128)S(1)} %copy-done.3) | data formatting | bytes 4194304
Async XLA Ops:
  69.8 1.6 %copy-start = (f32[128,4,1024]{2,1,0:T(4,128)S(1)}, f32[128,4,1024]{2,1,0:T(4,128)}, u32[]{:S(2)}) copy-start(f32[128,4,1024]{2,1,0:T(4,128)} %params_hbm.3) | copy-start | bytes 6291460
  71.4 1.6 %copy-start.1 = (f32[128,4,1024]{2,1,0:T(4,128)S(1)}, f32[128,4,1024]{2,1,0:T(4,128)}, u32[]{:S(2)}) copy-start(f32[128,4,1024]{2,1,0:T(4,128)} %get-tuple-element.6.theirs_hbm) | copy-start | bytes 6291460
  73.0 1.0 %copy-start.2 = (f32[256,384]{1,0:T(8,128)S(1)}, f32[256,384]{1,0:T(8,128)}, u32[]{:S(2)}) copy-start(f32[256,384]{1,0:T(8,128)} %get-tuple-element.5.sums) | copy-start | bytes 1179652
  74.0 21.6 %copy-start.3 = (f32[128,4,1024]{2,1,0:T(4,128)S(1)}, f32[128,4,1024]{2,1,0:T(4,128)}, u32[]{:S(2)}) copy-start(f32[128,4,1024]{2,1,0:T(4,128)} %get-tuple-element.11) | copy-start | bytes 6291460
